TPU v7x, 32 devices: a whole 2x2x4 slice. The times are simulated.
32 devices in a mesh: groups: 2 (over x), gz: 8 (over z, y), gy: 2 (over core).
Axes of the slice: x: 2, y: 2, z: 4, core: 2. Of those that a mesh axis runs over, the one named last changes fastest.
Arguments:
- momentum: float32 [3, 64, 64, 1024], P(None, ('groups', 'gz'), 'gy'), parts along dimension 1, may hold values from -4 to 4
- template: float32 [64, 64, 1024], P(('groups', 'gz'), 'gy'), parts along dimension 0, may hold values from -6 to 6
- target: float32 [64, 64, 1024], P(('groups', 'gz'), 'gy'), parts along dimension 0, may hold values from -6 to 6
Outputs:
- momentum_out: float32 [3, 64, 64, 1024], P(None, ('groups', 'gz'), 'gy'), parts along dimension 1
- deformed: float32 [64, 64, 1024], P(('groups', 'gz'), 'gy'), parts along dimension 0
- gradient: float32 [3, 64, 64, 1024], P(None, ('groups', 'gz'), 'gy'), parts along dimension 1
There are 2 independent parts, one for each index of `groups`. A program takes and returns all parts, laid end to end along the dimension named above; each array names one. Nothing has to cross between parts.
All inputs are finite; a program needn't handle non-finite values.
Results may differ from a plain program's by a relative error of at most 0.00002.
Values sent between devices are 32-bit elements; how exact they have to be, the bound alone decides.
A program may use at most 64 MiB of HBM per device.

v0:
```python
import jax
import jax.numpy as jnp
from jax import lax
from jax.sharding import PartitionSpec as P

STEPS = 2


TAPS = (0.05, 0.1, 0.2, 0.3, 0.2, 0.1, 0.05)
STEP_SIZE = 0.25


def extended(cells, sides, width):
    for axis, dim in sides:
        count = lax.axis_size(axis)
        ends = count - 1
        head = lax.slice_in_dim(cells, 0, width, axis=dim)
        tail = lax.slice_in_dim(cells, cells.shape[dim] - width, cells.shape[dim], axis=dim)
        cells = jnp.concatenate(
            [
                lax.ppermute(tail, axis, [(i, (i + 1) % count) for i in range(ends)]),
                cells,
                lax.ppermute(head, axis, [((i + 1) % count, i) for i in range(ends)]),
            ],
            axis=dim,
        )
    return cells


def taps_sum(padded, axis, length):
    total = jnp.zeros(padded.shape[:axis] + (length,) + padded.shape[axis + 1 :], jnp.float32)
    for k in range(7):
        total = total + TAPS[k] * lax.slice_in_dim(padded, k, k + length, axis=axis)
    return total


def pad_axis(field, axis, width):
    widths = [(0, 0)] * field.ndim
    widths[axis] = (width, width)
    return jnp.pad(field, widths)


def window(padded, axis, offset):
    out = padded
    for ax in (1, 2, 3):
        start = 1 + (offset if ax == axis else 0)
        out = lax.slice_in_dim(out, start, start + padded.shape[ax] - 2, axis=ax)
    return out


def advance(state_pad, velo_pad):
    state = window(state_pad, 0, 0)
    velo = window(velo_pad, 0, 0)
    advect = jnp.zeros_like(state)
    divergence = jnp.zeros_like(state[0])
    stretch = []
    for comp in range(3):
        axis = 3 - comp
        lower = window(state_pad, axis, -1)
        upper = window(state_pad, axis, 1)
        speed = velo[comp][None]
        advect = (
            advect
            + jnp.maximum(speed, 0.0) * (state - lower)
            + jnp.minimum(speed, 0.0) * (upper - state)
        )
        slope = 0.5 * (window(velo_pad, axis, 1) - window(velo_pad, axis, -1))
        divergence = divergence + slope[comp]
        stretch.append(state[0] * slope[0] + state[1] * slope[1] + state[2] * slope[2])
    moment = state[:3] - STEP_SIZE * (
        advect[:3] + jnp.stack(stretch) + state[:3] * divergence[None]
    )
    image = state[3:] - STEP_SIZE * advect[3:]
    return jnp.concatenate([moment, image], axis=0)


def source(state, image_pad, target):
    residual_img = state[3] - target
    forces = []
    for comp in range(3):
        axis = 3 - comp
        slope = 0.5 * (window(image_pad, axis, 1) - window(image_pad, axis, -1))[0]
        forces.append(state[comp] - residual_img * slope)
    return jnp.stack(forces)


def smooth_field(field):
    planes, rows, width = (field.shape[1], field.shape[2], field.shape[3])
    field = taps_sum(pad_axis(field, 3, 3), 3, width)
    field = taps_sum(extended(field, (("gy", 2),), 3), 2, rows)
    field = taps_sum(extended(field, (("gz", 1),), 3), 1, planes)
    return field


def on_device(momentum, template, target):
    state = jnp.concatenate([momentum, template[None]], axis=0)
    for step in range(STEPS):
        velo = smooth_field(state[:3])
        state_pad = pad_axis(extended(state, (("gz", 1), ("gy", 2)), 1), 3, 1)
        velo_pad = pad_axis(extended(velo, (("gz", 1), ("gy", 2)), 1), 3, 1)
        state = advance(state_pad, velo_pad)
    image_pad = pad_axis(extended(state[3:], (("gz", 1), ("gy", 2)), 1), 3, 1)
    gradient = smooth_field(source(state, image_pad, target))
    return (state[:3], state[3], gradient)


def solution(mesh):
    return jax.shard_map(
        on_device,
        mesh=mesh,
        in_specs=(
            P(None, ("groups", "gz"), "gy", None),
            P(("groups", "gz"), "gy", None),
            P(("groups", "gz"), "gy", None),
        ),
        out_specs=(
            P(None, ("groups", "gz"), "gy", None),
            P(("groups", "gz"), "gy", None),
            P(None, ("groups", "gz"), "gy", None),
        ),
        check_vma=False,
    )
```

profile of v0, /device:TPU:9, one launch (start us, length us, event | category | flops | bytes accessed | tf_op | source)
XLA Modules:
  0.0 347.4 jit_solution(15317008506014479708)
XLA Ops:
  0.6 7.9 %fusion.42 = f32[3,4,32,1024]{3,2,1,0:T(8,128)S(1)} fusion(f32[3,4,32,1024]{3,2,1,0:T(8,128)} %param.3), kind=kLoop, calls=%fused_computation.166 | loop fusion | flops 5111808 | bytes 3145728 | tf_op jit(solution)/shard_map/add | solution.py:33
  9.9 3.0 collective-permute-start.1
  13.1 3.1 collective-permute-start.4
  16.3 3.0 collective-permute-start.5
  21.0 18.1 %collective-permute-done.4 = f32[4,1,32,1024]{3,2,1,0:T(8,128)S(1)} collective-permute-done((f32[4,1,32,1024]{3,2,1,0:T(8,128)S(1)}, f32[4,1,32,1024]{3,2,1,0:T(8,128)S(1)}, u32[]{:S(2)}, u32[]{:S(2)}) %collective-permute-start.4) | collective-permute-done | bytes 524320 | tf_op jit(solution)/shard_map/ppermute | solution.py:21
  42.4 3.0 collective-permute-start.7
  47.9 4.1 %collective-permute-start.3 = (f32[3,3,32,1024]{3,2,1,0:T(8,128)S(1)}, f32[3,3,32,1024]{3,2,1,0:T(8,128)S(1)}, u32[]{:S(2)}, u32[]{:S(2)}) collective-permute-start(f32[3,3,32,1024]{3,2,1,0:T(8,128)S(1)} %get-tuple-element.53), channel_id=1, source_target_pairs={{2,0},{4,2},{6,4},{8,6},{10,8},{12,10},{14,12},{3,1},{5,3},{7,5},{... | collective-permute-start | bytes 3538952 | tf_op jit(solution)/shard_map/ppermute | solution.py:23
  52.0 4.5 %select_maximum_fusion.5 = f32[4,6,34,1026]{3,2,1,0:T(8,128)S(1)} fusion(f32[4,6,1,1024]{3,2,1,0:T(1,128)S(1)} %collective-permute-done.7, f32[4,6,1,1024]{3,2,1,0:T(1,128)S(1)} %collective-permute-done.6, f32[4,1,32,1024]{3,2,1,0:T(8,128)S(1)} %collective-permute-done.5, f32[4,1,32,1024]{3,2,1,0:T(8,128)S(1)} %collective-permute-done.4, ...), kind=kLoop, calls=%fused_computation.9 | loop fusion | flops 11721024 | bytes 6691200 | tf_op jit(solution)/shard_map/concatenate | solution.py:19
  56.5 42.3 %collective-permute-done.2 = f32[3,3,32,1024]{3,2,1,0:T(8,128)S(1)} collective-permute-done((f32[3,3,32,1024]{3,2,1,0:T(8,128)S(1)}, f32[3,3,32,1024]{3,2,1,0:T(8,128)S(1)}, u32[]{:S(2)}, u32[]{:S(2)}) %collective-permute-start.2) | collective-permute-done | bytes 1179680 | tf_op jit(solution)/shard_map/ppermute | solution.py:21
  105.4 4.3 %collective-permute-start.9 = (f32[3,1,32,1024]{3,2,1,0:T(8,128)S(1)}, f32[3,1,32,1024]{3,2,1,0:T(8,128)S(1)}, u32[]{:S(2)}, u32[]{:S(2)}) collective-permute-start(f32[3,1,32,1024]{3,2,1,0:T(8,128)S(1)} %get-tuple-element.44), channel_id=1, source_target_pairs={{2,0},{4,2},{6,4},{8,6},{10,8},{12,10},{14,12},{3,1},{5,3},{7,5},{... | collective-permute-start | bytes 1179656 | tf_op jit(solution)/shard_map/ppermute | solution.py:23
  112.6 9.7 %collective-permute-done.8 = f32[3,1,32,1024]{3,2,1,0:T(8,128)S(1)} collective-permute-done((f32[3,1,32,1024]{3,2,1,0:T(8,128)S(1)}, f32[3,1,32,1024]{3,2,1,0:T(8,128)S(1)}, u32[]{:S(2)}, u32[]{:S(2)}) %collective-permute-start.8) | collective-permute-done | bytes 393248 | tf_op jit(solution)/shard_map/ppermute | solution.py:21
  122.3 3.5 %collective-permute-done.9 = f32[3,1,32,1024]{3,2,1,0:T(8,128)S(1)} collective-permute-done((f32[3,1,32,1024]{3,2,1,0:T(8,128)S(1)}, f32[3,1,32,1024]{3,2,1,0:T(8,128)S(1)}, u32[]{:S(2)}, u32[]{:S(2)}) %collective-permute-start.9) | collective-permute-done | bytes 393248 | tf_op jit(solution)/shard_map/ppermute | solution.py:23
  127.2 3.2 collective-permute-start.11
  139.7 3.0 collective-permute-start.13
  144.7 4.3 %collective-permute-start.17 = (f32[4,1,32,1024]{3,2,1,0:T(8,128)S(1)}, f32[4,1,32,1024]{3,2,1,0:T(8,128)S(1)}, u32[]{:S(2)}, u32[]{:S(2)}) collective-permute-start(f32[4,1,32,1024]{3,2,1,0:T(8,128)S(1)} %get-tuple-element.19), channel_id=1, source_target_pairs={{2,0},{4,2},{6,4},{8,6},{10,8},{12,10},{14,12},{3,1},{5,3},{7,5},{... | collective-permute-start | bytes 1572872 | tf_op jit(solution)/shard_map/ppermute | solution.py:23
  150.7 16.5 %collective-permute-done.16 = f32[4,1,32,1024]{3,2,1,0:T(8,128)S(1)} collective-permute-done((f32[4,1,32,1024]{3,2,1,0:T(8,128)S(1)}, f32[4,1,32,1024]{3,2,1,0:T(8,128)S(1)}, u32[]{:S(2)}, u32[]{:S(2)}) %collective-permute-start.16) | collective-permute-done | bytes 524320 | tf_op jit(solution)/shard_map/ppermute | solution.py:21
  167.3 3.4 collective-permute-done.17
  172.1 3.0 collective-permute-start.19
  177.3 4.3 %collective-permute-start.15 = (f32[3,3,32,1024]{3,2,1,0:T(8,128)S(1)}, f32[3,3,32,1024]{3,2,1,0:T(8,128)S(1)}, u32[]{:S(2)}, u32[]{:S(2)}) collective-permute-start(f32[3,3,32,1024]{3,2,1,0:T(8,128)S(1)} %get-tuple-element.38), channel_id=1, source_target_pairs={{2,0},{4,2},{6,4},{8,6},{10,8},{12,10},{14,12},{3,1},{5,3},{7,5},{... | collective-permute-start | bytes 3538952 | tf_op jit(solution)/shard_map/ppermute | solution.py:23
  181.6 4.5 %select_maximum_fusion = f32[4,6,34,1026]{3,2,1,0:T(8,128)S(1)} fusion(f32[4,6,1,1024]{3,2,1,0:T(1,128)S(1)} %collective-permute-done.19, f32[4,6,1,1024]{3,2,1,0:T(1,128)S(1)} %collective-permute-done.18, f32[4,1,32,1024]{3,2,1,0:T(8,128)S(1)} %collective-permute-done.17, f32[4,1,32,1024]{3,2,1,0:T(8,128)S(1)} %collective-permute-done.16, ...), kind=kLoop, calls=%fused_computation.4 | loop fusion | flops 11721024 | bytes 6691200 | tf_op jit(solution)/shard_map/concatenate | solution.py:19
  186.1 41.8 %collective-permute-done.14 = f32[3,3,32,1024]{3,2,1,0:T(8,128)S(1)} collective-permute-done((f32[3,3,32,1024]{3,2,1,0:T(8,128)S(1)}, f32[3,3,32,1024]{3,2,1,0:T(8,128)S(1)}, u32[]{:S(2)}, u32[]{:S(2)}) %collective-permute-start.14) | collective-permute-done | bytes 1179680 | tf_op jit(solution)/shard_map/ppermute | solution.py:21
  227.9 3.4 collective-permute-done.15
  237.9 4.5 %collective-permute-start.21 = (f32[3,1,32,1024]{3,2,1,0:T(8,128)S(1)}, f32[3,1,32,1024]{3,2,1,0:T(8,128)S(1)}, u32[]{:S(2)}, u32[]{:S(2)}) collective-permute-start(f32[3,1,32,1024]{3,2,1,0:T(8,128)S(1)} %get-tuple-element.29), channel_id=1, source_target_pairs={{2,0},{4,2},{6,4},{8,6},{10,8},{12,10},{14,12},{3,1},{5,3},{7,5},{... | collective-permute-start | bytes 1179656 | tf_op jit(solution)/shard_map/ppermute | solution.py:23
  244.5 4.1 %collective-permute-start.25 = (f32[1,1,32,1024]{3,2,1,0:T(8,128)S(1)}, f32[1,1,32,1024]{3,2,1,0:T(8,128)S(1)}, u32[]{:S(2)}, u32[]{:S(2)}) collective-permute-start(f32[1,1,32,1024]{3,2,1,0:T(8,128)S(1)} %get-tuple-element.58), channel_id=1, source_target_pairs={{2,0},{4,2},{6,4},{8,6},{10,8},{12,10},{14,12},{3,1},{5,3},{7,5},{... | collective-permute-start | bytes 393224 | tf_op jit(solution)/shard_map/ppermute | solution.py:23
  248.6 11.7 %collective-permute-done.24 = f32[1,1,32,1024]{3,2,1,0:T(8,128)S(1)} collective-permute-done((f32[1,1,32,1024]{3,2,1,0:T(8,128)S(1)}, f32[1,1,32,1024]{3,2,1,0:T(8,128)S(1)}, u32[]{:S(2)}, u32[]{:S(2)}) %collective-permute-start.24) | collective-permute-done | bytes 131104 | tf_op jit(solution)/shard_map/ppermute | solution.py:21
  260.3 3.5 %collective-permute-done.25 = f32[1,1,32,1024]{3,2,1,0:T(8,128)S(1)} collective-permute-done((f32[1,1,32,1024]{3,2,1,0:T(8,128)S(1)}, f32[1,1,32,1024]{3,2,1,0:T(8,128)S(1)}, u32[]{:S(2)}, u32[]{:S(2)}) %collective-permute-start.25) | collective-permute-done | bytes 131104 | tf_op jit(solution)/shard_map/ppermute | solution.py:23
  265.2 3.0 collective-permute-start.27
  269.7 3.0 collective-permute-start.23
  283.3 3.0 collective-permute-start.29
  291.2 4.3 %collective-permute-start.31 = (f32[3,3,32,1024]{3,2,1,0:T(8,128)S(1)}, f32[3,3,32,1024]{3,2,1,0:T(8,128)S(1)}, u32[]{:S(2)}, u32[]{:S(2)}) collective-permute-start(f32[3,3,32,1024]{3,2,1,0:T(8,128)S(1)} %get-tuple-element.23), channel_id=1, source_target_pairs={{2,0},{4,2},{6,4},{8,6},{10,8},{12,10},{14,12},{3,1},{5,3},{7,5},{... | collective-permute-start | bytes 3538952 | tf_op jit(solution)/shard_map/ppermute | solution.py:23
  295.5 46.3 %collective-permute-done.30 = f32[3,3,32,1024]{3,2,1,0:T(8,128)S(1)} collective-permute-done((f32[3,3,32,1024]{3,2,1,0:T(8,128)S(1)}, f32[3,3,32,1024]{3,2,1,0:T(8,128)S(1)}, u32[]{:S(2)}, u32[]{:S(2)}) %collective-permute-start.30) | collective-permute-done | bytes 1179680 | tf_op jit(solution)/shard_map/ppermute | solution.py:21
  341.8 3.5 %collective-permute-done.31 = f32[3,3,32,1024]{3,2,1,0:T(8,128)S(1)} collective-permute-done((f32[3,3,32,1024]{3,2,1,0:T(8,128)S(1)}, f32[3,3,32,1024]{3,2,1,0:T(8,128)S(1)}, u32[]{:S(2)}, u32[]{:S(2)}) %collective-permute-start.31) | collective-permute-done | bytes 1179680 | tf_op jit(solution)/shard_map/ppermute | solution.py:23
  (89 shorter events, 65.0 us)
Async XLA Ops:
  8.6 10.7 %collective-permute-start = (f32[3,4,3,1024]{3,2,1,0:T(4,128)S(1)}, f32[3,4,3,1024]{3,2,1,0:T(4,128)S(1)}, u32[]{:S(2)}, u32[]{:S(2)}) collective-permute-start(f32[3,4,3,1024]{3,2,1,0:T(4,128)S(1)} %get-tuple-element.54), channel_id=1, source_target_pairs={{0,1},{2,3},{4,5},{6,7},{8,9},{10,11},{12,13},{14,15},{16,17},{18,... | collective-permute-start | bytes 442376 | tf_op jit(solution)/shard_map/ppermute | solution.py:21
  9.9 9.4 %collective-permute-start.1 = (f32[3,4,3,1024]{3,2,1,0:T(4,128)S(1)}, f32[3,4,3,1024]{3,2,1,0:T(4,128)S(1)}, u32[]{:S(2)}, u32[]{:S(2)}) collective-permute-start(f32[3,4,3,1024]{3,2,1,0:T(4,128)S(1)} %get-tuple-element.55), channel_id=1, source_target_pairs={{1,0},{3,2},{5,4},{7,6},{9,8},{11,10},{13,12},{15,14},{17,16},{19,... | collective-permute-start | bytes 442376 | tf_op jit(solution)/shard_map/ppermute | solution.py:23
  13.1 26.0 %collective-permute-start.4 = (f32[4,1,32,1024]{3,2,1,0:T(8,128)S(1)}, f32[4,1,32,1024]{3,2,1,0:T(8,128)S(1)}, u32[]{:S(2)}, u32[]{:S(2)}) collective-permute-start(f32[4,1,32,1024]{3,2,1,0:T(8,128)S(1)} %get-tuple-element.20), channel_id=1, source_target_pairs={{0,2},{2,4},{4,6},{6,8},{8,10},{10,12},{12,14},{1,3},{3,5},{5,7},{... | collective-permute-start | bytes 1572872 | tf_op jit(solution)/shard_map/ppermute | solution.py:21
  16.3 24.6 %collective-permute-start.5 = (f32[4,1,32,1024]{3,2,1,0:T(8,128)S(1)}, f32[4,1,32,1024]{3,2,1,0:T(8,128)S(1)}, u32[]{:S(2)}, u32[]{:S(2)}) collective-permute-start(f32[4,1,32,1024]{3,2,1,0:T(8,128)S(1)} %get-tuple-element.21), channel_id=1, source_target_pairs={{2,0},{4,2},{6,4},{8,6},{10,8},{12,10},{14,12},{3,1},{5,3},{7,5},{... | collective-permute-start | bytes 1572872 | tf_op jit(solution)/shard_map/ppermute | solution.py:23
  41.1 10.9 %collective-permute-start.6 = (f32[4,6,1,1024]{3,2,1,0:T(1,128)S(1)}, f32[4,6,1,1024]{3,2,1,0:T(1,128)S(1)}, u32[]{:S(2)}, u32[]{:S(2)}) collective-permute-start(f32[4,6,1,1024]{3,2,1,0:T(1,128)S(1)} %get-tuple-element.7), channel_id=1, source_target_pairs={{0,1},{2,3},{4,5},{6,7},{8,9},{10,11},{12,13},{14,15},{16,17},{18,... | collective-permute-start | bytes 294920 | tf_op jit(solution)/shard_map/ppermute | solution.py:21
  42.4 9.6 %collective-permute-start.7 = (f32[4,6,1,1024]{3,2,1,0:T(1,128)S(1)}, f32[4,6,1,1024]{3,2,1,0:T(1,128)S(1)}, u32[]{:S(2)}, u32[]{:S(2)}) collective-permute-start(f32[4,6,1,1024]{3,2,1,0:T(1,128)S(1)} %get-tuple-element.8), channel_id=1, source_target_pairs={{1,0},{3,2},{5,4},{7,6},{9,8},{11,10},{13,12},{15,14},{17,16},{19,... | collective-permute-start | bytes 294920 | tf_op jit(solution)/shard_map/ppermute | solution.py:23
  45.8 53.1 %collective-permute-start.2 = (f32[3,3,32,1024]{3,2,1,0:T(8,128)S(1)}, f32[3,3,32,1024]{3,2,1,0:T(8,128)S(1)}, u32[]{:S(2)}, u32[]{:S(2)}) collective-permute-start(f32[3,3,32,1024]{3,2,1,0:T(8,128)S(1)} %get-tuple-element.52), channel_id=1, source_target_pairs={{0,2},{2,4},{4,6},{6,8},{8,10},{10,12},{12,14},{1,3},{3,5},{5,7},{... | collective-permute-start | bytes 3538952 | tf_op jit(solution)/shard_map/ppermute | solution.py:21
  47.9 53.8 %collective-permute-start.3 = (f32[3,3,32,1024]{3,2,1,0:T(8,128)S(1)}, f32[3,3,32,1024]{3,2,1,0:T(8,128)S(1)}, u32[]{:S(2)}, u32[]{:S(2)}) collective-permute-start(f32[3,3,32,1024]{3,2,1,0:T(8,128)S(1)} %get-tuple-element.53), channel_id=1, source_target_pairs={{2,0},{4,2},{6,4},{8,6},{10,8},{12,10},{14,12},{3,1},{5,3},{7,5},{... | collective-permute-start | bytes 3538952 | tf_op jit(solution)/shard_map/ppermute | solution.py:23
  103.5 18.8 %collective-permute-start.8 = (f32[3,1,32,1024]{3,2,1,0:T(8,128)S(1)}, f32[3,1,32,1024]{3,2,1,0:T(8,128)S(1)}, u32[]{:S(2)}, u32[]{:S(2)}) collective-permute-start(f32[3,1,32,1024]{3,2,1,0:T(8,128)S(1)} %get-tuple-element.45), channel_id=1, source_target_pairs={{0,2},{2,4},{4,6},{6,8},{8,10},{10,12},{12,14},{1,3},{3,5},{5,7},{... | collective-permute-start | bytes 1179656 | tf_op jit(solution)/shard_map/ppermute | solution.py:21
  105.4 20.3 %collective-permute-start.9 = (f32[3,1,32,1024]{3,2,1,0:T(8,128)S(1)}, f32[3,1,32,1024]{3,2,1,0:T(8,128)S(1)}, u32[]{:S(2)}, u32[]{:S(2)}) collective-permute-start(f32[3,1,32,1024]{3,2,1,0:T(8,128)S(1)} %get-tuple-element.44), channel_id=1, source_target_pairs={{2,0},{4,2},{6,4},{8,6},{10,8},{12,10},{14,12},{3,1},{5,3},{7,5},{... | collective-permute-start | bytes 1179656 | tf_op jit(solution)/shard_map/ppermute | solution.py:23
  125.9 4.6 %collective-permute-start.10 = (f32[3,6,1,1024]{3,2,1,0:T(1,128)S(1)}, f32[3,6,1,1024]{3,2,1,0:T(1,128)S(1)}, u32[]{:S(2)}, u32[]{:S(2)}) collective-permute-start(f32[3,6,1,1024]{3,2,1,0:T(1,128)S(1)} %get-tuple-element.17), channel_id=1, source_target_pairs={{0,1},{2,3},{4,5},{6,7},{8,9},{10,11},{12,13},{14,15},{16,17},{18,... | collective-permute-start | bytes 221192 | tf_op jit(solution)/shard_map/ppermute | solution.py:21
  127.2 3.9 %collective-permute-start.11 = (f32[3,6,1,1024]{3,2,1,0:T(1,128)S(1)}, f32[3,6,1,1024]{3,2,1,0:T(1,128)S(1)}, u32[]{:S(2)}, u32[]{:S(2)}) collective-permute-start(f32[3,6,1,1024]{3,2,1,0:T(1,128)S(1)} %get-tuple-element.16), channel_id=1, source_target_pairs={{1,0},{3,2},{5,4},{7,6},{9,8},{11,10},{13,12},{15,14},{17,16},{19,... | collective-permute-start | bytes 221192 | tf_op jit(solution)/shard_map/ppermute | solution.py:23
  138.4 10.6 %collective-permute-start.12 = (f32[3,4,3,1024]{3,2,1,0:T(4,128)S(1)}, f32[3,4,3,1024]{3,2,1,0:T(4,128)S(1)}, u32[]{:S(2)}, u32[]{:S(2)}) collective-permute-start(f32[3,4,3,1024]{3,2,1,0:T(4,128)S(1)} %get-tuple-element.39), channel_id=1, source_target_pairs={{0,1},{2,3},{4,5},{6,7},{8,9},{10,11},{12,13},{14,15},{16,17},{18,... | collective-permute-start | bytes 442376 | tf_op jit(solution)/shard_map/ppermute | solution.py:21
  139.7 9.3 %collective-permute-start.13 = (f32[3,4,3,1024]{3,2,1,0:T(4,128)S(1)}, f32[3,4,3,1024]{3,2,1,0:T(4,128)S(1)}, u32[]{:S(2)}, u32[]{:S(2)}) collective-permute-start(f32[3,4,3,1024]{3,2,1,0:T(4,128)S(1)} %get-tuple-element.40), channel_id=1, source_target_pairs={{1,0},{3,2},{5,4},{7,6},{9,8},{11,10},{13,12},{15,14},{17,16},{19,... | collective-permute-start | bytes 442376 | tf_op jit(solution)/shard_map/ppermute | solution.py:23
  142.8 24.4 %collective-permute-start.16 = (f32[4,1,32,1024]{3,2,1,0:T(8,128)S(1)}, f32[4,1,32,1024]{3,2,1,0:T(8,128)S(1)}, u32[]{:S(2)}, u32[]{:S(2)}) collective-permute-start(f32[4,1,32,1024]{3,2,1,0:T(8,128)S(1)} %get-tuple-element.18), channel_id=1, source_target_pairs={{0,2},{2,4},{4,6},{6,8},{8,10},{10,12},{12,14},{1,3},{3,5},{5,7},{... | collective-permute-start | bytes 1572872 | tf_op jit(solution)/shard_map/ppermute | solution.py:21
  144.7 25.9 %collective-permute-start.17 = (f32[4,1,32,1024]{3,2,1,0:T(8,128)S(1)}, f32[4,1,32,1024]{3,2,1,0:T(8,128)S(1)}, u32[]{:S(2)}, u32[]{:S(2)}) collective-permute-start(f32[4,1,32,1024]{3,2,1,0:T(8,128)S(1)} %get-tuple-element.19), channel_id=1, source_target_pairs={{2,0},{4,2},{6,4},{8,6},{10,8},{12,10},{14,12},{3,1},{5,3},{7,5},{... | collective-permute-start | bytes 1572872 | tf_op jit(solution)/shard_map/ppermute | solution.py:23
  170.8 10.8 %collective-permute-start.18 = (f32[4,6,1,1024]{3,2,1,0:T(1,128)S(1)}, f32[4,6,1,1024]{3,2,1,0:T(1,128)S(1)}, u32[]{:S(2)}, u32[]{:S(2)}) collective-permute-start(f32[4,6,1,1024]{3,2,1,0:T(1,128)S(1)} %get-tuple-element.5), channel_id=1, source_target_pairs={{0,1},{2,3},{4,5},{6,7},{8,9},{10,11},{12,13},{14,15},{16,17},{18,... | collective-permute-start | bytes 294920 | tf_op jit(solution)/shard_map/ppermute | solution.py:21
  172.1 9.5 %collective-permute-start.19 = (f32[4,6,1,1024]{3,2,1,0:T(1,128)S(1)}, f32[4,6,1,1024]{3,2,1,0:T(1,128)S(1)}, u32[]{:S(2)}, u32[]{:S(2)}) collective-permute-start(f32[4,6,1,1024]{3,2,1,0:T(1,128)S(1)} %get-tuple-element.6), channel_id=1, source_target_pairs={{1,0},{3,2},{5,4},{7,6},{9,8},{11,10},{13,12},{15,14},{17,16},{19,... | collective-permute-start | bytes 294920 | tf_op jit(solution)/shard_map/ppermute | solution.py:23
  175.4 52.5 %collective-permute-start.14 = (f32[3,3,32,1024]{3,2,1,0:T(8,128)S(1)}, f32[3,3,32,1024]{3,2,1,0:T(8,128)S(1)}, u32[]{:S(2)}, u32[]{:S(2)}) collective-permute-start(f32[3,3,32,1024]{3,2,1,0:T(8,128)S(1)} %get-tuple-element.37), channel_id=1, source_target_pairs={{0,2},{2,4},{4,6},{6,8},{8,10},{10,12},{12,14},{1,3},{3,5},{5,7},{... | collective-permute-start | bytes 3538952 | tf_op jit(solution)/shard_map/ppermute | solution.py:21
  177.3 54.0 %collective-permute-start.15 = (f32[3,3,32,1024]{3,2,1,0:T(8,128)S(1)}, f32[3,3,32,1024]{3,2,1,0:T(8,128)S(1)}, u32[]{:S(2)}, u32[]{:S(2)}) collective-permute-start(f32[3,3,32,1024]{3,2,1,0:T(8,128)S(1)} %get-tuple-element.38), channel_id=1, source_target_pairs={{2,0},{4,2},{6,4},{8,6},{10,8},{12,10},{14,12},{3,1},{5,3},{7,5},{... | collective-permute-start | bytes 3538952 | tf_op jit(solution)/shard_map/ppermute | solution.py:23
  236.0 32.3 %collective-permute-start.20 = (f32[3,1,32,1024]{3,2,1,0:T(8,128)S(1)}, f32[3,1,32,1024]{3,2,1,0:T(8,128)S(1)}, u32[]{:S(2)}, u32[]{:S(2)}) collective-permute-start(f32[3,1,32,1024]{3,2,1,0:T(8,128)S(1)} %get-tuple-element.30), channel_id=1, source_target_pairs={{0,2},{2,4},{4,6},{6,8},{8,10},{10,12},{12,14},{1,3},{3,5},{5,7},{... | collective-permute-start | bytes 1179656 | tf_op jit(solution)/shard_map/ppermute | solution.py:21
  237.9 30.4 %collective-permute-start.21 = (f32[3,1,32,1024]{3,2,1,0:T(8,128)S(1)}, f32[3,1,32,1024]{3,2,1,0:T(8,128)S(1)}, u32[]{:S(2)}, u32[]{:S(2)}) collective-permute-start(f32[3,1,32,1024]{3,2,1,0:T(8,128)S(1)} %get-tuple-element.29), channel_id=1, source_target_pairs={{2,0},{4,2},{6,4},{8,6},{10,8},{12,10},{14,12},{3,1},{5,3},{7,5},{... | collective-permute-start | bytes 1179656 | tf_op jit(solution)/shard_map/ppermute | solution.py:23
  242.4 17.9 %collective-permute-start.24 = (f32[1,1,32,1024]{3,2,1,0:T(8,128)S(1)}, f32[1,1,32,1024]{3,2,1,0:T(8,128)S(1)}, u32[]{:S(2)}, u32[]{:S(2)}) collective-permute-start(f32[1,1,32,1024]{3,2,1,0:T(8,128)S(1)} %get-tuple-element.59), channel_id=1, source_target_pairs={{0,2},{2,4},{4,6},{6,8},{8,10},{10,12},{12,14},{1,3},{3,5},{5,7},{... | collective-permute-start | bytes 393224 | tf_op jit(solution)/shard_map/ppermute | solution.py:21
  244.5 19.4 %collective-permute-start.25 = (f32[1,1,32,1024]{3,2,1,0:T(8,128)S(1)}, f32[1,1,32,1024]{3,2,1,0:T(8,128)S(1)}, u32[]{:S(2)}, u32[]{:S(2)}) collective-permute-start(f32[1,1,32,1024]{3,2,1,0:T(8,128)S(1)} %get-tuple-element.58), channel_id=1, source_target_pairs={{2,0},{4,2},{6,4},{8,6},{10,8},{12,10},{14,12},{3,1},{5,3},{7,5},{... | collective-permute-start | bytes 393224 | tf_op jit(solution)/shard_map/ppermute | solution.py:23
  263.9 8.8 %collective-permute-start.26 = (f32[1,6,1,1024]{3,2,1,0:T(1,128)S(1)}, f32[1,6,1,1024]{3,2,1,0:T(1,128)S(1)}, u32[]{:S(2)}, u32[]{:S(2)}) collective-permute-start(f32[1,6,1,1024]{3,2,1,0:T(1,128)S(1)} %get-tuple-element.57), channel_id=1, source_target_pairs={{0,1},{2,3},{4,5},{6,7},{8,9},{10,11},{12,13},{14,15},{16,17},{18,... | collective-permute-start | bytes 73736 | tf_op jit(solution)/shard_map/ppermute | solution.py:21
  265.2 7.5 %collective-permute-start.27 = (f32[1,6,1,1024]{3,2,1,0:T(1,128)S(1)}, f32[1,6,1,1024]{3,2,1,0:T(1,128)S(1)}, u32[]{:S(2)}, u32[]{:S(2)}) collective-permute-start(f32[1,6,1,1024]{3,2,1,0:T(1,128)S(1)} %get-tuple-element.56), channel_id=1, source_target_pairs={{1,0},{3,2},{5,4},{7,6},{9,8},{11,10},{13,12},{15,14},{17,16},{19,... | collective-permute-start | bytes 73736 | tf_op jit(solution)/shard_map/ppermute | solution.py:23
  268.4 4.9 %collective-permute-start.22 = (f32[3,6,1,1024]{3,2,1,0:T(1,128)S(1)}, f32[3,6,1,1024]{3,2,1,0:T(1,128)S(1)}, u32[]{:S(2)}, u32[]{:S(2)}) collective-permute-start(f32[3,6,1,1024]{3,2,1,0:T(1,128)S(1)} %get-tuple-element.13), channel_id=1, source_target_pairs={{0,1},{2,3},{4,5},{6,7},{8,9},{10,11},{12,13},{14,15},{16,17},{18,... | collective-permute-start | bytes 221192 | tf_op jit(solution)/shard_map/ppermute | solution.py:21
  269.7 3.9 %collective-permute-start.23 = (f32[3,6,1,1024]{3,2,1,0:T(1,128)S(1)}, f32[3,6,1,1024]{3,2,1,0:T(1,128)S(1)}, u32[]{:S(2)}, u32[]{:S(2)}) collective-permute-start(f32[3,6,1,1024]{3,2,1,0:T(1,128)S(1)} %get-tuple-element.12), channel_id=1, source_target_pairs={{1,0},{3,2},{5,4},{7,6},{9,8},{11,10},{13,12},{15,14},{17,16},{19,... | collective-permute-start | bytes 221192 | tf_op jit(solution)/shard_map/ppermute | solution.py:23
  282.0 4.4 %collective-permute-start.28 = (f32[3,4,3,1024]{3,2,1,0:T(4,128)S(1)}, f32[3,4,3,1024]{3,2,1,0:T(4,128)S(1)}, u32[]{:S(2)}, u32[]{:S(2)}) collective-permute-start(f32[3,4,3,1024]{3,2,1,0:T(4,128)S(1)} %get-tuple-element.24), channel_id=1, source_target_pairs={{0,1},{2,3},{4,5},{6,7},{8,9},{10,11},{12,13},{14,15},{16,17},{18,... | collective-permute-start | bytes 442376 | tf_op jit(solution)/shard_map/ppermute | solution.py:21
  283.3 4.1 %collective-permute-start.29 = (f32[3,4,3,1024]{3,2,1,0:T(4,128)S(1)}, f32[3,4,3,1024]{3,2,1,0:T(4,128)S(1)}, u32[]{:S(2)}, u32[]{:S(2)}) collective-permute-start(f32[3,4,3,1024]{3,2,1,0:T(4,128)S(1)} %get-tuple-element.25), channel_id=1, source_target_pairs={{1,0},{3,2},{5,4},{7,6},{9,8},{11,10},{13,12},{15,14},{17,16},{19,... | collective-permute-start | bytes 442376 | tf_op jit(solution)/shard_map/ppermute | solution.py:23
  289.3 52.5 %collective-permute-start.30 = (f32[3,3,32,1024]{3,2,1,0:T(8,128)S(1)}, f32[3,3,32,1024]{3,2,1,0:T(8,128)S(1)}, u32[]{:S(2)}, u32[]{:S(2)}) collective-permute-start(f32[3,3,32,1024]{3,2,1,0:T(8,128)S(1)} %get-tuple-element.22), channel_id=1, source_target_pairs={{0,2},{2,4},{4,6},{6,8},{8,10},{10,12},{12,14},{1,3},{3,5},{5,7},{... | collective-permute-start | bytes 3538952 | tf_op jit(solution)/shard_map/ppermute | solution.py:21
  291.2 54.1 %collective-permute-start.31 = (f32[3,3,32,1024]{3,2,1,0:T(8,128)S(1)}, f32[3,3,32,1024]{3,2,1,0:T(8,128)S(1)}, u32[]{:S(2)}, u32[]{:S(2)}) collective-permute-start(f32[3,3,32,1024]{3,2,1,0:T(8,128)S(1)} %get-tuple-element.23), channel_id=1, source_target_pairs={{2,0},{4,2},{6,4},{8,6},{10,8},{12,10},{14,12},{3,1},{5,3},{7,5},{... | collective-permute-start | bytes 3538952 | tf_op jit(solution)/shard_map/ppermute | solution.py:23
  (5 other events, 68.6 us)
where the time goes:
time: 348 us; the launch traced here: 347 us
  waiting for transfers between devices  210 us (60%)
  starting transfers between devices  84.5 us (24%)
  other arithmetic  48.7 us (14%)
    ppermute x16, waiting for transfers between devices, extended(): lax.ppermute(tail, axis, [(i, (i + 1) % count) for i in range(ends)])  187 us
    ppermute x16, starting transfers between devices, extended(): lax.ppermute(head, axis, [((i + 1) % count, i) for i in range(ends)])  57.3 us
    ppermute x16, starting transfers between devices, extended(): lax.ppermute(tail, axis, [(i, (i + 1) % count) for i in range(ends)])  27.2 us
    ppermute x16, waiting for transfers between devices, extended(): lax.ppermute(head, axis, [((i + 1) % count, i) for i in range(ends)])  23.9 us
    add x9, other arithmetic, taps_sum(): total = total + TAPS[k] * lax.slice_in_dim(padded, k, k + length, axis=axis)  22.6 us
    concatenate x8, other arithmetic, extended(): jnp.concatenate([lax.ppermute(tail, axis, [(i, (i + 1) % count) for i in...  12.7 us
  transfers between devices with their start and end apart: 32, of which 17 were waited for; matrix products, arithmetic and copies ran while one was open for 5% of the time, Pallas kernels for 0%

commit v1 on v0

v1 whole, which is shorter than its diff:
```python
import functools

import jax
import jax.numpy as jnp
from jax import lax
from jax.experimental import pallas as pl
from jax.experimental.pallas import tpu as pltpu
from jax.sharding import PartitionSpec as P

STEPS = 2
TAPS = (0.05, 0.1, 0.2, 0.3, 0.2, 0.1, 0.05)
STEP_SIZE = 0.25
LANES = 128
SUB = 8


def taps7(load):
    return (
        TAPS[3] * load(0)
        + TAPS[2] * (load(-1) + load(1))
        + TAPS[1] * (load(-2) + load(2))
        + TAPS[0] * (load(-3) + load(3))
    )


def kernel(
    n, ny, half,
    m_hbm, i_hbm, t_hbm, mo_hbm, io_hbm, go_hbm,
    M0, M1, A, V, I0, I1, D, T, Q, M2, G,
    send_sem, recv_sem, loc_sem,
):
    g = lax.axis_index("gz")
    c = lax.axis_index("gy")
    p = lax.rem(g, 2)
    slab = lax.div(g, 2)
    nslab = n // 2
    partner = g + 1 - 2 * p
    depth = m_hbm.shape[1]
    planes = 2 * depth
    rows = m_hbm.shape[2]
    high = rows + 2 * SUB
    wide = half + LANES
    has_dn, has_up = slab > 0, slab < nslab - 1
    has_yl, has_yh = c > 0, c < ny - 1
    mid = slice(SUB, SUB + rows)

    count = [0, 0]

    def z_dev(d):
        return {"gz": d}

    def y_dev(d):
        return {"gy": d}

    class Copy:
        def __init__(self, src, dst, dev, sends=None, gets=None):
            k = count[0]
            count[0] += 1
            self.c = pltpu.make_async_remote_copy(
                src_ref=src, dst_ref=dst, send_sem=send_sem.at[k], recv_sem=recv_sem.at[k],
                device_id=dev, device_id_type=pl.DeviceIdType.MESH,
            )
            self.sends, self.gets = sends, gets

        def _do(self, cond, f):
            if cond is None:
                f()
            else:
                pl.when(cond)(f)

        def start(self):
            self._do(self.sends, self.c.start)
            return self

        def arrive(self):
            self._do(self.gets, self.c.wait_recv)

        def sent(self):
            self._do(self.sends, self.c.wait_send)

    def local(src, dst):
        k = count[1]
        count[1] += 1
        cp = pltpu.make_async_copy(src, dst, loc_sem.at[k])
        cp.start()
        return cp

    done = []

    barrier = pltpu.get_barrier_semaphore()

    def greet(dev):
        pl.semaphore_signal(barrier, inc=1, device_id=dev, device_id_type=pl.DeviceIdType.MESH)

    greet(z_dev(partner))
    for cond, dev in (
        (has_dn, z_dev(g - 2)), (has_up, z_dev(g + 2)), (has_yl, y_dev(c - 1)), (has_yh, y_dev(c + 1)),
    ):
        pl.when(cond)(functools.partial(greet, dev))
    friends = 1 + sum(jnp.where(cond, 1, 0) for cond in (has_dn, has_up, has_yl, has_yh))

    win = pl.multiple_of(p * (half - LANES), LANES)
    win_other = pl.multiple_of((1 - p) * (half - LANES), LANES)

    loc = [local(m_hbm.at[j, :, :, pl.ds(win, wide)], M0.at[j, pl.ds(4 + depth * p, depth), mid]) for j in range(3)]
    loc_i = local(i_hbm.at[:, :, pl.ds(win, wide)], I0.at[pl.ds(2 + depth * p, depth), mid])
    loc_t = local(t_hbm.at[:, :, pl.ds(win, wide)], T.at[pl.ds(depth * p, depth)])

    def blank(ref, *idx):
        ref[idx] = jnp.zeros(ref.at[idx].shape, jnp.float32)

    def blank_z(ref, lead, lo, hi):
        @pl.when(jnp.logical_not(has_dn))
        def _():
            blank(ref, *lead, slice(0, lo), mid)

        @pl.when(jnp.logical_not(has_up))
        def _():
            blank(ref, *lead, slice(hi, None), mid)

        @pl.when(jnp.logical_not(has_yl))
        def _():
            blank(ref, *lead, slice(None), slice(0, SUB))

        @pl.when(jnp.logical_not(has_yh))
        def _():
            blank(ref, *lead, slice(None), slice(SUB + rows, None))

    every = slice(None)
    pl.semaphore_wait(barrier, friends)

    out_dev = z_dev(g - 2 + 4 * p)
    in_dev = z_dev(g + 2 - 4 * p)
    odd = p == 1
    out_sends = jnp.logical_or(jnp.logical_and(odd, has_up), jnp.logical_and(p == 0, has_dn))
    out_gets = jnp.logical_or(jnp.logical_and(odd, has_dn), jnp.logical_and(p == 0, has_up))
    swaps, outs, ins = [], [], []
    for j in range(3):
        swaps.append(
            Copy(m_hbm.at[j, :, :, pl.ds(win_other, wide)], M0.at[j, pl.ds(4 + depth * p, depth), mid], z_dev(partner)).start()
        )
        outs.append(
            Copy(m_hbm.at[j, pl.ds((depth - 4) * p, 4), :, pl.ds(win, wide)], M0.at[j, pl.ds((planes + 4) * (1 - p), 4), mid], out_dev, out_sends, out_gets).start()
        )
    swap_i = Copy(i_hbm.at[:, :, pl.ds(win_other, wide)], I0.at[pl.ds(2 + depth * p, depth), mid], z_dev(partner)).start()
    out_i = Copy(
        i_hbm.at[pl.ds((depth - 1) * p, 1), :, pl.ds(win, wide)], I0.at[pl.ds(2 + planes - (planes + 1) * p, 1), mid], out_dev, out_sends, out_gets
    ).start()
    swap_t = Copy(t_hbm.at[:, :, pl.ds(win_other, wide)], T.at[pl.ds(depth * p, depth)], z_dev(partner)).start()

    blank_z(M0, (every,), 4, 4 + planes)
    blank_z(M1, (every,), 4, 4 + planes)
    blank_z(I0, (), 2, 2 + planes)
    blank_z(I1, (), 2, 2 + planes)
    blank_z(Q, (every,), 3, 3 + planes)

    def y_faces(view):
        lo = Copy(view(slice(SUB, 2 * SUB)), view(slice(SUB + rows, high)), y_dev(c - 1), has_yl, has_yh).start()
        hi = Copy(view(slice(rows, rows + SUB)), view(slice(0, SUB)), y_dev(c + 1), has_yh, has_yl).start()
        done.extend([lo, hi])
        return lo, hi

    for j in range(3):
        swaps[j].arrive()
        ins.append(
            Copy(
                M0.at[j, pl.ds(planes - (planes - 4) * p, 4), mid], M0.at[j, pl.ds((planes + 4) * p, 4), mid], in_dev, out_gets, out_sends
            ).start()
        )
    swap_i.arrive()
    in_i = Copy(
        I0.at[pl.ds(1 + planes - (planes - 1) * p, 1), mid], I0.at[pl.ds(1 + (planes + 1) * p, 1), mid], in_dev, out_gets, out_sends
    ).start()

    lane = lax.broadcasted_iota(jnp.int32, (SUB, wide), 1)
    keep = jnp.where(odd, lane, wide - 1 - lane) >= 3

    def keep_rows(r):
        return jnp.where(odd, lax.broadcasted_iota(jnp.int32, (r, wide), 1), wide - 1 - lax.broadcasted_iota(jnp.int32, (r, wide), 1)) >= 3

    def roll(f, s, axis):
        return pltpu.roll(f, s % f.shape[axis], axis)

    def smooth_xy(ref, j, depth_):
        def body(z, _):
            for t in range(high // SUB):
                f = jnp.where(keep, ref[j, z, t * SUB : (t + 1) * SUB], 0.0)
                A[j, z, t * SUB : (t + 1) * SUB] = taps7(lambda k: f if k == 0 else roll(f, -k, 1))
            f = A[j, z]
            for b in range(wide // LANES):
                s = f[:, b * LANES : (b + 1) * LANES]
                A[j, z, :, b * LANES : (b + 1) * LANES] = taps7(lambda k: s if k == 0 else roll(s, -k, 0))
            return 0

        lax.fori_loop(0, depth_, body, 0)

    zlast = planes + 1

    def outside(z, t, f):
        ok = jnp.logical_and(jnp.logical_or(z > 0, has_dn), jnp.logical_or(z < zlast, has_up))
        if t == 0:
            ok = jnp.logical_and(ok, has_yl)
        if t == high // SUB - 1:
            ok = jnp.logical_and(ok, has_yh)
        return f * jnp.where(ok, 1.0, 0.0)

    def smooth_z_velo(j):
        def body(z, _):
            for t in range(high // SUB):
                rs = slice(t * SUB, (t + 1) * SUB)
                f = taps7(lambda k: A[j, z + k + 3, rs])
                V[j, z, rs] = outside(z, t, jnp.where(keep, f, 0.0))
            return 0

        lax.fori_loop(0, planes + 2, body, 0)

    def around(load, z, t):
        lo, hi = max(0, (t - 1) * SUB), min(high, (t + 2) * SUB)
        tall = load(z, slice(lo, hi))
        at = slice(t * SUB - lo, t * SUB - lo + SUB)
        f = tall[at]
        rs = slice(t * SUB, (t + 1) * SUB)
        return f, (
            (roll(f, 1, 1), roll(f, -1, 1)),
            (roll(tall, 1, 0)[at], roll(tall, -1, 0)[at]),
            (load(z - 1, rs), load(z + 1, rs)),
        )

    def reader(ref, *lead):
        def load(z, rs):
            f = ref[(*lead, z, rs)]
            return jnp.where(keep_rows(f.shape[0]), f, 0.0)

        return load

    def plain(ref, *lead):
        return lambda z, rs: ref[(*lead, z, rs)]

    def advect(pos, neg, f, near):
        total = 0.0
        for i in range(3):
            total = total + pos[i] * (f - near[i][0]) + neg[i] * (near[i][1] - f)
        return total

    tiles = range(1, 1 + rows // SUB)

    def advance(Mi, zs, store):
        def body(z, _):
            for t in tiles:
                mids, nears = zip(*(around(reader(Mi, j), z + 4, t) for j in range(3)))
                v, vn = zip(*(around(plain(V, j), z + 1, t) for j in range(3)))
                pos = [jnp.maximum(u, 0.0) for u in v]
                neg = [jnp.minimum(u, 0.0) for u in v]
                div = 0.5 * sum(vn[i][i][1] - vn[i][i][0] for i in range(3))
                for j in range(3):
                    stretch = 0.5 * sum(mids[i] * (vn[i][j][1] - vn[i][j][0]) for i in range(3))
                    new = mids[j] - STEP_SIZE * (advect(pos, neg, mids[j], nears[j]) + stretch + mids[j] * div)
                    store(j, z, t, new)
            return 0

        lax.fori_loop(zs[0], zs[1], body, 0)

    def advance_image(Ii, z0, z1, ts, store):
        def body(z, _):
            for t in ts:
                f, near = around(reader(Ii), z + 1, t)
                v = [V[j, z, t * SUB : (t + 1) * SUB] for j in range(3)]
                pos = [jnp.maximum(u, 0.0) for u in v]
                neg = [jnp.minimum(u, 0.0) for u in v]
                store(z, t, f - STEP_SIZE * advect(pos, neg, f, near))
            return 0

        lax.fori_loop(z0, z1, body, 0)

    def tile(t):
        return slice(t * SUB, (t + 1) * SUB)

    for j in range(3):
        loc[j].wait()
        outs[j].arrive()
        ins[j].arrive()
        y_m = y_faces(lambda r: M0.at[j, :, r])
        if j == 0:
            loc_i.wait()
            out_i.arrive()
            in_i.arrive()
            y_i = y_faces(lambda r: I0.at[:, r])
        for f in y_m:
            f.arrive()
        smooth_xy(M0, j, planes + 8)
        smooth_z_velo(j)
    for f in y_i:
        f.arrive()

    def store_m1(j, z, t, f):
        M1[j, z + 4, tile(t)] = f

    def store_i1(z, t, f):
        I1[z + 1, tile(t)] = f

    dn, up = z_dev(g - 2), z_dev(g + 2)
    advance(M0, (0, 4), store_m1)
    go = [Copy(M1.at[j, 4:8, mid], M1.at[j, planes + 4 : planes + 8, mid], dn, has_dn, has_up).start() for j in range(3)]
    advance(M0, (planes - 4, planes), store_m1)
    gu = [Copy(M1.at[j, planes : planes + 4, mid], M1.at[j, 0:4, mid], up, has_up, has_dn).start() for j in range(3)]
    advance_image(I0, 1, planes + 1, tiles, store_i1)
    go_i = Copy(I1.at[2:4, mid], I1.at[planes + 2 : planes + 4, mid], dn, has_dn, has_up).start()
    gu_i = Copy(I1.at[planes : planes + 2, mid], I1.at[0:2, mid], up, has_up, has_dn).start()
    done.extend(swaps + outs + ins + [swap_i, out_i, in_i, swap_t] + go + gu + [go_i, gu_i])

    for j in range(3):
        go[j].arrive()
        gu[j].arrive()
        for f in y_faces(lambda r: M1.at[j, :, r]):
            f.arrive()
        smooth_xy(M1, j, planes + 8)
        smooth_z_velo(j)
    go_i.arrive()
    gu_i.arrive()
    y_i = y_faces(lambda r: I1.at[:, r])

    def store_m2(j, z, t, f):
        M2[j, z, (t - 1) * SUB : t * SUB] = f

    def store_i2(z, t, f):
        D[z, tile(t)] = outside(z, t, f)

    advance(M1, (0, planes), store_m2)
    for f in y_i:
        f.arrive()
    advance_image(I1, 0, planes + 2, range(high // SUB), store_i2)

    lanes_in = pl.ds(pl.multiple_of(LANES * p, LANES), half)
    lanes_out = pl.ds(pl.multiple_of(half * p, LANES), half)
    mine, theirs = pl.ds(depth * p, depth), pl.ds(depth * (1 - p), depth)
    locs = []

    def give(src, dst):
        done.append(Copy(src(theirs), dst, z_dev(partner)).start())
        locs.append(local(src(mine), dst))

    loc_t.wait()
    swap_t.arrive()

    def force(z0, z1):
        def body(z, _):
            for t in tiles:
                f, near = around(reader(D), z + 1, t)
                res = (f - T[z, (t - 1) * SUB : t * SUB]) * 0.5
                for j in range(3):
                    Q[j, z + 3, tile(t)] = M2[j, z, (t - 1) * SUB : t * SUB] - res * (near[j][1] - near[j][0])
            return 0

        lax.fori_loop(z0, z1, body, 0)

    force(0, 3)
    go = [Copy(Q.at[j, 3:6, mid], Q.at[j, planes + 3 : planes + 6, mid], dn, has_dn, has_up).start() for j in range(3)]
    force(planes - 3, planes)
    gu = [Copy(Q.at[j, planes : planes + 3, mid], Q.at[j, 0:3, mid], up, has_up, has_dn).start() for j in range(3)]
    force(3, planes - 3)
    done.extend(go + gu)
    for j in range(3):
        give(lambda z: M2.at[j, z, :, lanes_in], mo_hbm.at[j, :, :, lanes_out])

    def d_planes(z):
        return D.at[pl.ds(z.start + 1, depth), mid, lanes_in]

    give(d_planes, io_hbm.at[:, :, lanes_out])

    for j in range(3):
        go[j].arrive()
        gu[j].arrive()
        for f in y_faces(lambda r: Q.at[j, :, r]):
            f.arrive()
        smooth_xy(Q, j, planes + 6)

        def body(z, _):
            for t in tiles:
                G[j, z, (t - 1) * SUB : t * SUB] = taps7(lambda k: A[j, z + k + 3, tile(t)])
            return 0

        lax.fori_loop(0, planes, body, 0)
        give(lambda z: G.at[j, z, :, lanes_in], go_hbm.at[j, :, :, lanes_out])

    for f in done:
        f.sent()
    for f in done:
        if f.gets is None and f not in swaps and f is not swap_i and f is not swap_t:
            f.arrive()
    for f in locs:
        f.wait()


def solution(mesh):
    n, ny = mesh.shape["gz"], mesh.shape["gy"]

    def on_device(momentum, template, target):
        _, depth, rows, full = momentum.shape
        half = full // 2
        planes, high, wide = 2 * depth, rows + 2 * SUB, half + LANES

        def buf(*lead):
            return pltpu.VMEM((*lead, wide), jnp.float32)

        return pl.pallas_call(
            functools.partial(kernel, n, ny, half),
            out_shape=tuple(jax.ShapeDtypeStruct(a.shape, a.dtype) for a in (momentum, template, momentum)),
            in_specs=[pl.BlockSpec(memory_space=pl.ANY)] * 3,
            out_specs=[pl.BlockSpec(memory_space=pl.ANY)] * 3,
            scratch_shapes=[
                buf(3, planes + 8, high),
                buf(3, planes + 8, high),
                buf(3, planes + 8, high),
                buf(3, planes + 2, high),
                buf(planes + 4, high),
                buf(planes + 4, high),
                buf(planes + 2, high),
                buf(planes, rows),
                buf(3, planes + 6, high),
                buf(3, planes, rows),
                buf(3, planes, rows),
                pltpu.SemaphoreType.DMA((80,)),
                pltpu.SemaphoreType.DMA((80,)),
                pltpu.SemaphoreType.DMA((16,)),
            ],
            compiler_params=pltpu.CompilerParams(
                collective_id=0, has_side_effects=True, vmem_limit_bytes=56 * 1024 * 1024
            ),
        )(momentum, template, target)

    return jax.shard_map(
        on_device,
        mesh=mesh,
        in_specs=(
            P(None, ("groups", "gz"), "gy", None),
            P(("groups", "gz"), "gy", None),
            P(("groups", "gz"), "gy", None),
        ),
        out_specs=(
            P(None, ("groups", "gz"), "gy", None),
            P(("groups", "gz"), "gy", None),
            P(None, ("groups", "gz"), "gy", None),
        ),
        check_vma=False,
    )
```

time: 348 us -> 146 us (0.42)
  waiting for transfers between devices: 210 us -> 0 us
  Pallas kernels: 0 us -> 140 us
  starting transfers between devices: 84.5 us -> 0 us
  other arithmetic: 48.7 us -> 0 us
    ppermute x32 -> x0, waiting for transfers between devices: 210 us -> none  [the longest x16 187 us: extended(): lax.ppermute(tail, axis, [(i, (i + 1) % count) for i in range(ends)])]
    pallas_call x0 -> x1, Pallas kernels: none -> 140 us  [on_device(): pl.pallas_call(functools.partial(kernel, n, ny, half), out_shape=tuple((j...]
    ppermute x32 -> x0, starting transfers between devices: 84.5 us -> none  [the longest x16 57.3 us: extended(): lax.ppermute(head, axis, [((i + 1) % count, i) for i in range(ends)])]
    add x13 -> x0, other arithmetic: 28.9 us -> none  [the longest x9 22.6 us: taps_sum(): total = total + TAPS[k] * lax.slice_in_dim(padded, k, k + length, axis=axis)]
    concatenate x10 -> x0, other arithmetic: 12.9 us -> none  [the longest x8 12.7 us: extended(): jnp.concatenate([lax.ppermute(tail, axis, [(i, (i + 1) % count) for i in...]
    mul x7 -> x0, other arithmetic: 4.6 us -> none  [the longest x3 2.52 us: advance(): slope = 0.5 * (window(velo_pad, axis, 1) - window(velo_pad, axis, -1))]
    unnamed x10 -> x7, local copies, waits for them, and re-layouts: 1.13 us -> 4.82 us
  transfers between devices with their start and end apart: 32 -> 0, of which waited for: 17 -> 0; matrix products, arithmetic and copies ran while one was open for 5% -> 0% of each run, Pallas kernels for 0% -> 0%
where the time goes in v1:
time: 146 us; the launch traced here: 145 us
  Pallas kernels  140 us (96%)
  local copies, waits for them, and re-layouts  4.82 us (3%)
    pallas_call x1, Pallas kernels, on_device(): pl.pallas_call(functools.partial(kernel, n, ny, half), out_shape=tuple((j...  140 us
    unnamed x7, local copies, waits for them, and re-layouts  4.82 us

profile of v1, /device:TPU:9, one launch (start us, length us, event | category | flops | bytes accessed | tf_op | source)
XLA Modules:
  0.0 145.2 jit_solution(9879706844034244167)
XLA Ops:
  0.6 139.7 %shard_map.58 = (f32[3,4,32,1024]{3,2,1,0:T(8,128)}, f32[4,32,1024]{2,1,0:T(8,128)}, f32[3,4,32,1024]{3,2,1,0:T(8,128)}) custom-call(f32[3,4,32,1024]{3,2,1,0:T(8,128)} %m_hbm.1, f32[4,32,1024]{2,1,0:T(8,128)} %i_hbm.1, f32[4,32,1024]{2,1,0:T(8,128)} %t_hbm.1), custom_call_target="tpu_custom_call" | custom-call | tf_op jit(solution)/shard_map/pallas_call | solution.py:405
  140.4 0.0 copy-start.1
  140.4 0.0 copy-start
  140.4 2.9 %copy.9 = f32[3,4,32,1024]{3,2,1,0:T(8,128)} copy(f32[3,4,32,1024]{3,2,1,0:T(8,128)} %get-tuple-element.6) | data formatting | bytes 3145728
  143.3 0.0 copy-done.1
  143.3 0.8 copy.10
  144.1 0.0 copy-done
  144.1 1.1 copy.11
Async XLA Ops:
  140.4 2.9 %copy-start.1 = (f32[4,32,1024]{2,1,0:T(8,128)S(1)}, f32[4,32,1024]{2,1,0:T(8,128)}, u32[]{:S(2)}) copy-start(f32[4,32,1024]{2,1,0:T(8,128)} %get-tuple-element.7) | copy-start | bytes 1572868
  140.4 3.7 %copy-start = (f32[3,4,32,1024]{3,2,1,0:T(8,128)S(1)}, f32[3,4,32,1024]{3,2,1,0:T(8,128)}, u32[]{:S(2)}) copy-start(f32[3,4,32,1024]{3,2,1,0:T(8,128)} %get-tuple-element.8) | copy-start | bytes 4718596

commit v2 on v1

--- a/solution.py
+++ b/solution.py
@@ -142,11 +142,11 @@
         outs.append(
             Copy(m_hbm.at[j, pl.ds((depth - 4) * p, 4), :, pl.ds(win, wide)], M0.at[j, pl.ds((planes + 4) * (1 - p), 4), mid], out_dev, out_sends, out_gets).start()
         )
-    swap_i = Copy(i_hbm.at[:, :, pl.ds(win_other, wide)], I0.at[pl.ds(2 + depth * p, depth), mid], z_dev(partner)).start()
+    swap_i = Copy(i_hbm.at[:, :, pl.ds(win_other, wide)], I0.at[pl.ds(2 + depth * p, depth), mid], z_dev(partner))
     out_i = Copy(
         i_hbm.at[pl.ds((depth - 1) * p, 1), :, pl.ds(win, wide)], I0.at[pl.ds(2 + planes - (planes + 1) * p, 1), mid], out_dev, out_sends, out_gets
     ).start()
-    swap_t = Copy(t_hbm.at[:, :, pl.ds(win_other, wide)], T.at[pl.ds(depth * p, depth)], z_dev(partner)).start()
+    swap_t = Copy(t_hbm.at[:, :, pl.ds(win_other, wide)], T.at[pl.ds(depth * p, depth)], z_dev(partner))
 
     blank_z(M0, (every,), 4, 4 + planes)
     blank_z(M1, (every,), 4, 4 + planes)
@@ -167,10 +167,10 @@
                 M0.at[j, pl.ds(planes - (planes - 4) * p, 4), mid], M0.at[j, pl.ds((planes + 4) * p, 4), mid], in_dev, out_gets, out_sends
             ).start()
         )
-    swap_i.arrive()
+    swap_i.start()
     in_i = Copy(
         I0.at[pl.ds(1 + planes - (planes - 1) * p, 1), mid], I0.at[pl.ds(1 + (planes + 1) * p, 1), mid], in_dev, out_gets, out_sends
-    ).start()
+    )
 
     lane = lax.broadcasted_iota(jnp.int32, (SUB, wide), 1)
     keep = jnp.where(odd, lane, wide - 1 - lane) >= 3
@@ -178,18 +178,24 @@
     def keep_rows(r):
         return jnp.where(odd, lax.broadcasted_iota(jnp.int32, (r, wide), 1), wide - 1 - lax.broadcasted_iota(jnp.int32, (r, wide), 1)) >= 3
 
+    keep_all = keep_rows(high)
+
     def roll(f, s, axis):
         return pltpu.roll(f, s % f.shape[axis], axis)
 
-    def smooth_xy(ref, j, depth_):
+    def taps_cyclic(f, axis):
+        u = 2.0 * f + (roll(f, 1, axis) + roll(f, -1, axis))
+        return TAPS[0] * (3.0 * u + (roll(u, 2, axis) + roll(u, -2, axis)))
+
+    def smooth(ref, j, depth_, store):
         def body(z, _):
             for t in range(high // SUB):
-                f = jnp.where(keep, ref[j, z, t * SUB : (t + 1) * SUB], 0.0)
-                A[j, z, t * SUB : (t + 1) * SUB] = taps7(lambda k: f if k == 0 else roll(f, -k, 1))
-            f = A[j, z]
+                rs = slice(t * SUB, (t + 1) * SUB)
+                f = jnp.where(keep, taps7(lambda k: ref[j, z + k + 3, rs]), 0.0)
+                A[rs] = taps_cyclic(f, 1)
             for b in range(wide // LANES):
-                s = f[:, b * LANES : (b + 1) * LANES]
-                A[j, z, :, b * LANES : (b + 1) * LANES] = taps7(lambda k: s if k == 0 else roll(s, -k, 0))
+                ls = slice(b * LANES, (b + 1) * LANES)
+                store(z, ls, taps_cyclic(A[:, ls], 0))
             return 0
 
         lax.fori_loop(0, depth_, body, 0)
@@ -204,15 +210,19 @@
             ok = jnp.logical_and(ok, has_yh)
         return f * jnp.where(ok, 1.0, 0.0)
 
-    def smooth_z_velo(j):
-        def body(z, _):
-            for t in range(high // SUB):
-                rs = slice(t * SUB, (t + 1) * SUB)
-                f = taps7(lambda k: A[j, z + k + 3, rs])
-                V[j, z, rs] = outside(z, t, jnp.where(keep, f, 0.0))
-            return 0
-
-        lax.fori_loop(0, planes + 2, body, 0)
+    row = lax.broadcasted_iota(jnp.int32, (high, LANES), 0)
+
+    def smooth_velo(ref, j):
+        def store(z, ls, f):
+            ok = jnp.logical_and(jnp.logical_or(z > 0, has_dn), jnp.logical_or(z < zlast, has_up))
+            lo = jnp.where(has_yl, 0, SUB)
+            hi = jnp.where(ok, jnp.where(has_yh, high, SUB + rows), 0)
+            inside = jnp.logical_and(row >= lo, row < hi)
+            if ls.start == 0 or ls.stop == wide:
+                inside = jnp.logical_and(inside, keep_all[:, ls])
+            V[j, z, :, ls] = jnp.where(inside, f, 0.0)
+
+        smooth(ref, j, planes + 2, store)
 
     def around(load, z, t):
         lo, hi = max(0, (t - 1) * SUB), min(high, (t + 2) * SUB)
@@ -279,18 +289,17 @@
         loc[j].wait()
         outs[j].arrive()
         ins[j].arrive()
-        y_m = y_faces(lambda r: M0.at[j, :, r])
+        for f in y_faces(lambda r: M0.at[j, :, r]):
+            f.arrive()
+        smooth_velo(M0, j)
         if j == 0:
-            loc_i.wait()
-            out_i.arrive()
-            in_i.arrive()
-            y_i = y_faces(lambda r: I0.at[:, r])
-        for f in y_m:
-            f.arrive()
-        smooth_xy(M0, j, planes + 8)
-        smooth_z_velo(j)
-    for f in y_i:
-        f.arrive()
+            swap_i.arrive()
+            in_i.start()
+            swap_t.start()
+    loc_i.wait()
+    out_i.arrive()
+    in_i.arrive()
+    y_i = y_faces(lambda r: I0.at[:, r])
 
     def store_m1(j, z, t, f):
         M1[j, z + 4, tile(t)] = f
@@ -303,6 +312,9 @@
     go = [Copy(M1.at[j, 4:8, mid], M1.at[j, planes + 4 : planes + 8, mid], dn, has_dn, has_up).start() for j in range(3)]
     advance(M0, (planes - 4, planes), store_m1)
     gu = [Copy(M1.at[j, planes : planes + 4, mid], M1.at[j, 0:4, mid], up, has_up, has_dn).start() for j in range(3)]
+    own = [y_faces(lambda r: M1.at[j, 4 : 4 + planes, r]) for j in range(3)]
+    for f in y_i:
+        f.arrive()
     advance_image(I0, 1, planes + 1, tiles, store_i1)
     go_i = Copy(I1.at[2:4, mid], I1.at[planes + 2 : planes + 4, mid], dn, has_dn, has_up).start()
     gu_i = Copy(I1.at[planes : planes + 2, mid], I1.at[0:2, mid], up, has_up, has_dn).start()
@@ -311,10 +323,10 @@
     for j in range(3):
         go[j].arrive()
         gu[j].arrive()
-        for f in y_faces(lambda r: M1.at[j, :, r]):
+        ends = y_faces(lambda r: M1.at[j, 0:4, r]) + y_faces(lambda r: M1.at[j, 4 + planes : 8 + planes, r])
+        for f in own[j] + ends:
             f.arrive()
-        smooth_xy(M1, j, planes + 8)
-        smooth_z_velo(j)
+        smooth_velo(M1, j)
     go_i.arrive()
     gu_i.arrive()
     y_i = y_faces(lambda r: I1.at[:, r])
@@ -324,11 +336,6 @@
 
     def store_i2(z, t, f):
         D[z, tile(t)] = outside(z, t, f)
-
-    advance(M1, (0, planes), store_m2)
-    for f in y_i:
-        f.arrive()
-    advance_image(I1, 0, planes + 2, range(high // SUB), store_i2)
 
     lanes_in = pl.ds(pl.multiple_of(LANES * p, LANES), half)
     lanes_out = pl.ds(pl.multiple_of(half * p, LANES), half)
@@ -338,6 +345,16 @@
     def give(src, dst):
         done.append(Copy(src(theirs), dst, z_dev(partner)).start())
         locs.append(local(src(mine), dst))
+
+    def d_planes(z):
+        return D.at[pl.ds(z.start + 1, depth), mid, lanes_in]
+
+    advance(M1, (0, planes), store_m2)
+    for j in range(3):
+        give(lambda z: M2.at[j, z, :, lanes_in], mo_hbm.at[j, :, :, lanes_out])
+    for f in y_i:
+        f.arrive()
+    advance_image(I1, 0, planes + 2, range(high // SUB), store_i2)
 
     loc_t.wait()
     swap_t.arrive()
@@ -358,28 +375,21 @@
     force(planes - 3, planes)
     gu = [Copy(Q.at[j, planes : planes + 3, mid], Q.at[j, 0:3, mid], up, has_up, has_dn).start() for j in range(3)]
     force(3, planes - 3)
+    own = [y_faces(lambda r: Q.at[j, 3 : 3 + planes, r]) for j in range(3)]
     done.extend(go + gu)
-    for j in range(3):
-        give(lambda z: M2.at[j, z, :, lanes_in], mo_hbm.at[j, :, :, lanes_out])
-
-    def d_planes(z):
-        return D.at[pl.ds(z.start + 1, depth), mid, lanes_in]
-
     give(d_planes, io_hbm.at[:, :, lanes_out])
 
     for j in range(3):
         go[j].arrive()
         gu[j].arrive()
-        for f in y_faces(lambda r: Q.at[j, :, r]):
+        ends = y_faces(lambda r: Q.at[j, 0:3, r]) + y_faces(lambda r: Q.at[j, 3 + planes : 6 + planes, r])
+        for f in own[j] + ends:
             f.arrive()
-        smooth_xy(Q, j, planes + 6)
-
-        def body(z, _):
-            for t in tiles:
-                G[j, z, (t - 1) * SUB : t * SUB] = taps7(lambda k: A[j, z + k + 3, tile(t)])
-            return 0
-
-        lax.fori_loop(0, planes, body, 0)
+
+        def store_g(z, ls, f):
+            G[j, z, :, ls] = f[mid]
+
+        smooth(Q, j, planes, store_g)
         give(lambda z: G.at[j, z, :, lanes_in], go_hbm.at[j, :, :, lanes_out])
 
     for f in done:
@@ -410,7 +420,7 @@
             scratch_shapes=[
                 buf(3, planes + 8, high),
                 buf(3, planes + 8, high),
-                buf(3, planes + 8, high),
+                buf(high),
                 buf(3, planes + 2, high),
                 buf(planes + 4, high),
                 buf(planes + 4, high),
@@ -419,8 +429,8 @@
                 buf(3, planes + 6, high),
                 buf(3, planes, rows),
                 buf(3, planes, rows),
-                pltpu.SemaphoreType.DMA((80,)),
-                pltpu.SemaphoreType.DMA((80,)),
+                pltpu.SemaphoreType.DMA((96,)),
+                pltpu.SemaphoreType.DMA((96,)),
                 pltpu.SemaphoreType.DMA((16,)),
             ],
             compiler_params=pltpu.CompilerParams(

time: 146 us -> 125 us (0.86)
  Pallas kernels: 140 us -> 119 us
    pallas_call x1, Pallas kernels: 140 us -> 119 us  [on_device(): pl.pallas_call(functools.partial(kernel, n, ny, half), out_shape=tuple((j...]
where the time goes in v2:
time: 125 us
  Pallas kernels  119 us (95%)
  local copies, waits for them, and re-layouts  4.82 us (4%)
    pallas_call x1, Pallas kernels, on_device(): pl.pallas_call(functools.partial(kernel, n, ny, half), out_shape=tuple((j...  119 us
    unnamed x7, local copies, waits for them, and re-layouts  4.82 us

profile of v2, /device:TPU:9, one launch (start us, length us, event | category | flops | bytes accessed | tf_op | source)
XLA Modules:
  0.0 124.7 jit_solution(1209053384568857242)
XLA Ops:
  0.6 119.2 %shard_map.58 = (f32[3,4,32,1024]{3,2,1,0:T(8,128)}, f32[4,32,1024]{2,1,0:T(8,128)}, f32[3,4,32,1024]{3,2,1,0:T(8,128)}) custom-call(f32[3,4,32,1024]{3,2,1,0:T(8,128)} %m_hbm.1, f32[4,32,1024]{2,1,0:T(8,128)} %i_hbm.1, f32[4,32,1024]{2,1,0:T(8,128)} %t_hbm.1), custom_call_target="tpu_custom_call" | custom-call | tf_op jit(solution)/shard_map/pallas_call | solution.py:415
  119.8 0.0 copy-start.1
  119.8 0.0 copy-start
  119.8 2.9 %copy.9 = f32[3,4,32,1024]{3,2,1,0:T(8,128)} copy(f32[3,4,32,1024]{3,2,1,0:T(8,128)} %get-tuple-element.6) | data formatting | bytes 3145728
  122.7 0.0 copy-done.1
  122.7 0.8 copy.10
  123.5 0.0 copy-done
  123.5 1.1 copy.11
Async XLA Ops:
  119.8 2.9 %copy-start.1 = (f32[4,32,1024]{2,1,0:T(8,128)S(1)}, f32[4,32,1024]{2,1,0:T(8,128)}, u32[]{:S(2)}) copy-start(f32[4,32,1024]{2,1,0:T(8,128)} %get-tuple-element.7) | copy-start | bytes 1572868
  119.8 3.7 %copy-start = (f32[3,4,32,1024]{3,2,1,0:T(8,128)S(1)}, f32[3,4,32,1024]{3,2,1,0:T(8,128)}, u32[]{:S(2)}) copy-start(f32[3,4,32,1024]{3,2,1,0:T(8,128)} %get-tuple-element.8) | copy-start | bytes 4718596
